TPU v7x, 128 devices: a whole 4x4x4 slice. The times are simulated.
128 devices in a mesh: shard: 32 (over z, y, core), grp: 4 (over x).
Axes of the slice: x: 4, y: 4, z: 4, core: 2. Of those that a mesh axis runs over, the one named last changes fastest.
Arguments:
- embeddings: bfloat16 [98304, 1024], P(('shard', 'grp'))
- worker: int32 [98304], P(('shard', 'grp')), may hold values from 0 to 127, as said below
- label: int32 [98304], P(('shard', 'grp')), may hold values from 0 to 1, as said below
Outputs:
- nearest_similarity: float32 [98304], P(('shard', 'grp'))
Inputs may be any that keep to these rules, and one draw needn't show every extreme that they name: Among the rows of one device at most 12 name the same worker; some workers are named by exactly 12 rows of every device. Among the rows of one device at most 6 name the same worker and label. Rows with equal worker and label form one cluster of at most 768 rows; some cluster holds exactly 768.
All inputs are finite; a program needn't handle non-finite values.
Results may differ from a plain program's by a relative error of at most 0.00054.
Values may be sent and summed in bfloat16 or wider, within the bound.
No kernel may reach another device: no remote copies, remote signals or barrier semaphores. Data moves between devices by JAX's collectives and lax.ppermute only.
A program may use at most 64 MiB of HBM per device.

v0:
```python
import jax
import jax.numpy as jnp
from jax import lax
from jax.sharding import PartitionSpec as P

SUB = 2


def score_full(incoming, filled):
    cluster_rows = incoming.shape[1]
    tile_rows = 256
    tile_count = cluster_rows // tile_rows
    column_list = jnp.arange(cluster_rows, dtype=jnp.int32)

    def one_tile(flat_index):
        group_index = flat_index // tile_count
        first_row = flat_index % tile_count * tile_rows
        members = incoming[group_index]
        member_fill = filled[group_index]
        block = lax.dynamic_slice_in_dim(members, first_row, tile_rows, 0)
        block_fill = lax.dynamic_slice_in_dim(member_fill, first_row, tile_rows, 0)
        scores = lax.dot_general(
            block, members, (((1,), (1,)), ((), ())), preferred_element_type=jnp.float32
        )
        positions = first_row + jnp.arange(tile_rows, dtype=jnp.int32)
        same = (block_fill[:, None] > 0) & (member_fill[None, :] > 0)
        same = same & (positions[:, None] != column_list[None, :])
        return jnp.max(jnp.where(same, scores, -4.0), axis=1)

    group_count = incoming.shape[0]
    best_score = lax.map(one_tile, jnp.arange(group_count * tile_count, dtype=jnp.int32))
    best_score = best_score.reshape(group_count, cluster_rows)
    return jnp.where(best_score < -2.0, -1.0, best_score)


def local(embeddings, worker, label):
    width = embeddings.shape[1]
    row_count = embeddings.shape[0]
    partition_count = lax.axis_size("shard")
    group_count = lax.axis_size("grp")
    devices = partition_count * group_count
    per_worker = 2 * row_count // devices
    per_label = per_worker // SUB
    values = embeddings.astype(jnp.float32)
    unit = (values * lax.rsqrt(jnp.sum(values * values, axis=1, keepdims=True) + 1e-06)).astype(
        jnp.bfloat16
    )
    local_cluster = worker * SUB + label
    onehot = (local_cluster[:, None] == jnp.arange(devices * SUB, dtype=jnp.int32)[None, :]).astype(
        jnp.int32
    )
    earlier = jnp.cumsum(onehot, axis=0) - onehot
    rank_within = jnp.sum(earlier * onehot, axis=1)
    slot_index = local_cluster * per_label + rank_within
    outgoing = jnp.zeros((devices * SUB * per_label, width), jnp.bfloat16).at[slot_index].set(unit)
    out_fill = jnp.zeros((devices * SUB * per_label,), jnp.int32).at[slot_index].set(1)
    incoming, inbound_fill = (
        lax.all_to_all(
            outgoing.reshape(devices, SUB, 1, per_label, width),
            ("shard", "grp"),
            split_axis=0,
            concat_axis=2,
            tiled=True,
        ),
        lax.all_to_all(
            out_fill.reshape(devices, SUB, 1, per_label),
            ("shard", "grp"),
            split_axis=0,
            concat_axis=2,
            tiled=True,
        ),
    )
    incoming = incoming.reshape(SUB, devices * per_label, width)
    inbound_fill = inbound_fill.reshape(SUB, devices * per_label)
    best_score = score_full(incoming, inbound_fill)
    returned = lax.all_to_all(
        best_score.reshape(SUB, devices, per_label),
        ("shard", "grp"),
        split_axis=1,
        concat_axis=0,
        tiled=True,
    )
    return returned.reshape(devices * SUB * per_label)[slot_index]


def solution(mesh):
    return jax.shard_map(
        local,
        mesh=mesh,
        in_specs=(P(("shard", "grp"), None), P(("shard", "grp")), P(("shard", "grp"))),
        out_specs=P(("shard", "grp")),
        check_vma=False,
    )
```

profile of v0, /device:TPU:1, one launch (start us, length us, event | category | flops | bytes accessed | tf_op | source)
XLA Modules:
  0.0 145.6 jit_solution(5029110283193673635)
XLA Ops:
  0.0 0.7 multiply_add_fusion
  0.7 0.1 copy.10
  0.8 0.0 copy-start
  0.8 0.2 fusion.21
  1.1 0.1 broadcast_add_fusion
  1.1 0.3 copy.11
  1.4 0.3 fusion.24
  1.7 3.4 %scatter_custom_fusion = s32[1536]{0:T(1024)S(1)} fusion(s32[768]{0:T(1024)S(1)} %compare_select_fusion.1, s32[768]{0:T(1024)S(1)} %broadcast.62, s32[]{:T(128)} %constant.157.clone.1), kind=kCustom, calls=%fused_computation.39 | custom fusion | bytes 6148 | tf_op jit(solution)/shard_map/scatter | solution.py:56
  5.1 0.9 reshape.78
  6.0 11.5 %all-to-all-start = ((s32[128,2,1,6]{3,1,2,0:T(2,128)}), s32[128,2,1,6]{3,1,2,0:T(2,128)S(1)}, u32[]{:S(2)}, u32[]{:S(2)}) async-start(s32[128,2,1,6]{3,1,2,0:T(2,128)} %bitcast.4), calls=%async_computation | async-start | bytes 262144 | tf_op jit(solution)/shard_map/all_to_all | solution.py:65
  17.5 0.0 copy-done
  17.5 0.4 fusion.15
  17.9 10.6 %scatter_custom_fusion.1 = bf16[1536,1024]{1,0:T(8,128)(2,1)S(1)} fusion(s32[768]{0:T(1024)S(1)} %compare_select_fusion.1, bf16[768,1024]{1,0:T(8,128)(2,1)} %param.5, f32[768]{0:T(1024)S(1)} %add_rsqrt_fusion, bf16[]{:T(256)} %constant.159.clone.1), kind=kCustom, calls=%fused_computation.21 | custom fusion | flops 2359296 | bytes 4722690 | tf_op jit(solution)/shard_map/scatter | solution.py:55
  28.5 2.9 %reshape.80 = bf16[128,2,1,6,1024]{4,3,1,0,2:T(8,128)(2,1)} reshape(bf16[1536,1024]{1,0:T(8,128)(2,1)S(1)} %scatter_custom_fusion.1) | data formatting | bytes 6291456 | tf_op jit(solution)/shard_map/reshape | solution.py:59
  31.4 10.2 %copy.14 = bf16[128,2,1,6,1024]{4,1,3,2,0:T(2,128)(2,1)} copy(bf16[128,2,1,6,1024]{4,3,1,0,2:T(8,128)(2,1)} %reshape.80) | data formatting | bytes 6291456 | tf_op jit(solution)/shard_map/reshape | solution.py:59
  41.6 0.0 all-to-all-done
  41.6 9.8 %all-to-all-start.1 = ((bf16[128,2,1,6,1024]{4,1,3,2,0:T(2,128)(2,1)}), bf16[128,2,1,6,1024]{4,1,3,2,0:T(2,128)(2,1)S(1)}, u32[]{:S(2)}, u32[]{:S(2)}) async-start(bf16[128,2,1,6,1024]{4,1,3,2,0:T(2,128)(2,1)} %copy.14), calls=%async_computation.1 | async-start | bytes 6291456 | tf_op jit(solution)/shard_map/all_to_all | solution.py:58
  51.4 0.1 reshape.79
  51.5 41.9 %all-to-all-done.1 = bf16[128,2,1,6,1024]{4,1,3,2,0:T(2,128)(2,1)S(1)} async-done(((bf16[128,2,1,6,1024]{4,1,3,2,0:T(2,128)(2,1)}), bf16[128,2,1,6,1024]{4,1,3,2,0:T(2,128)(2,1)S(1)}, u32[]{:S(2)}, u32[]{:S(2)}) %all-to-all-start.1) | async-done | bytes 3145760 | tf_op jit(solution)/shard_map/all_to_all | solution.py:58
  93.4 2.6 %copy.15 = bf16[2,768,1024]{2,1,0:T(8,128)(2,1)} copy(bf16[2,768,1024]{2,0,1:T(2,128)(2,1)S(1)} %bitcast.56) | data formatting | bytes 6291456
  96.0 28.5 %while.14 = (s32[]{:T(128)}, f32[6,256]{1,0:T(8,128)S(1)}, s32[6]{0:T(128)S(1)}, s32[2,768]{1,0:T(2,128)S(1)}, bf16[2,768,1024]{2,1,0:T(8,128)(2,1)}, /*index=5*...) while((s32[]{:T(128)}, f32[6,256]{1,0:T(8,128)S(1)}, ...), condition=%wide.region_8.9_spmd.clone, body=%wide.region_6.8_spmd.clone.sunk | while | flops 403637280 | bytes 2108828 | solution.py:31
  96.0 0.6 dynamic_slice.59
  98.3 0.1 compare_reduce_fusion.5
  98.4 2.3 %fusion.33 = f32[256]{0:T(256)S(1)} fusion(bf16[2,768,1024]{2,1,0:T(8,128)(2,1)} %get-tuple-element.212, s32[]{:T(128)S(6)} %select_n.82, s32[]{:T(128)S(6)} %select_n.83, s32[]{:T(128)S(6)} %select_n.86, s32[256]{0:T(256)S(1)} %iota_add_fusion.2, pred[768]{0:T(1024)(128)(4,1)S(1)} %compare_reduce_fusion.4, pred[256]{0:T(512)(128)(4,1)S(1)} %compare_reduce_fusion.5), kind=kOutput, calls=%fused_computation.8.clone.1 | convolution fusion | flops 403635968 | bytes 2100236 | tf_op jit(solution)/shard_map/while/body/eval_jaxpr/dot_general | solution.py:22
  100.8 0.6 dynamic_slice.59
  103.0 0.1 compare_reduce_fusion.5
  103.2 2.3 %fusion.33 = f32[256]{0:T(256)S(1)} fusion(bf16[2,768,1024]{2,1,0:T(8,128)(2,1)} %get-tuple-element.212, s32[]{:T(128)S(6)} %select_n.82, s32[]{:T(128)S(6)} %select_n.83, s32[]{:T(128)S(6)} %select_n.86, s32[256]{0:T(256)S(1)} %iota_add_fusion.2, pred[768]{0:T(1024)(128)(4,1)S(1)} %compare_reduce_fusion.4, pred[256]{0:T(512)(128)(4,1)S(1)} %compare_reduce_fusion.5), kind=kOutput, calls=%fused_computation.8.clone.1 | convolution fusion | flops 403635968 | bytes 2100236 | tf_op jit(solution)/shard_map/while/body/eval_jaxpr/dot_general | solution.py:22
  105.5 0.6 dynamic_slice.59
  107.8 0.1 compare_reduce_fusion.5
  107.9 2.3 %fusion.33 = f32[256]{0:T(256)S(1)} fusion(bf16[2,768,1024]{2,1,0:T(8,128)(2,1)} %get-tuple-element.212, s32[]{:T(128)S(6)} %select_n.82, s32[]{:T(128)S(6)} %select_n.83, s32[]{:T(128)S(6)} %select_n.86, s32[256]{0:T(256)S(1)} %iota_add_fusion.2, pred[768]{0:T(1024)(128)(4,1)S(1)} %compare_reduce_fusion.4, pred[256]{0:T(512)(128)(4,1)S(1)} %compare_reduce_fusion.5), kind=kOutput, calls=%fused_computation.8.clone.1 | convolution fusion | flops 403635968 | bytes 2100236 | tf_op jit(solution)/shard_map/while/body/eval_jaxpr/dot_general | solution.py:22
  110.3 0.6 dynamic_slice.59
  112.5 0.1 compare_reduce_fusion.5
  112.7 2.3 %fusion.33 = f32[256]{0:T(256)S(1)} fusion(bf16[2,768,1024]{2,1,0:T(8,128)(2,1)} %get-tuple-element.212, s32[]{:T(128)S(6)} %select_n.82, s32[]{:T(128)S(6)} %select_n.83, s32[]{:T(128)S(6)} %select_n.86, s32[256]{0:T(256)S(1)} %iota_add_fusion.2, pred[768]{0:T(1024)(128)(4,1)S(1)} %compare_reduce_fusion.4, pred[256]{0:T(512)(128)(4,1)S(1)} %compare_reduce_fusion.5), kind=kOutput, calls=%fused_computation.8.clone.1 | convolution fusion | flops 403635968 | bytes 2100236 | tf_op jit(solution)/shard_map/while/body/eval_jaxpr/dot_general | solution.py:22
  115.0 0.6 dynamic_slice.59
  117.3 0.1 compare_reduce_fusion.5
  117.4 2.3 %fusion.33 = f32[256]{0:T(256)S(1)} fusion(bf16[2,768,1024]{2,1,0:T(8,128)(2,1)} %get-tuple-element.212, s32[]{:T(128)S(6)} %select_n.82, s32[]{:T(128)S(6)} %select_n.83, s32[]{:T(128)S(6)} %select_n.86, s32[256]{0:T(256)S(1)} %iota_add_fusion.2, pred[768]{0:T(1024)(128)(4,1)S(1)} %compare_reduce_fusion.4, pred[256]{0:T(512)(128)(4,1)S(1)} %compare_reduce_fusion.5), kind=kOutput, calls=%fused_computation.8.clone.1 | convolution fusion | flops 403635968 | bytes 2100236 | tf_op jit(solution)/shard_map/while/body/eval_jaxpr/dot_general | solution.py:22
  119.8 0.6 dynamic_slice.59
  122.0 0.1 compare_reduce_fusion.5
  122.1 2.3 %fusion.33 = f32[256]{0:T(256)S(1)} fusion(bf16[2,768,1024]{2,1,0:T(8,128)(2,1)} %get-tuple-element.212, s32[]{:T(128)S(6)} %select_n.82, s32[]{:T(128)S(6)} %select_n.83, s32[]{:T(128)S(6)} %select_n.86, s32[256]{0:T(256)S(1)} %iota_add_fusion.2, pred[768]{0:T(1024)(128)(4,1)S(1)} %compare_reduce_fusion.4, pred[256]{0:T(512)(128)(4,1)S(1)} %compare_reduce_fusion.5), kind=kOutput, calls=%fused_computation.8.clone.1 | convolution fusion | flops 403635968 | bytes 2100236 | tf_op jit(solution)/shard_map/while/body/eval_jaxpr/dot_general | solution.py:22
  124.5 0.1 reshape.82
  124.7 0.7 copy.16
  125.4 3.8 %all-to-all-start.2 = ((f32[2,128,6]{2,0,1:T(2,128)}), f32[2,128,6]{2,0,1:T(2,128)S(1)}, u32[]{:S(2)}, u32[]{:S(2)}) async-start(f32[2,128,6]{2,0,1:T(2,128)} %copy.16), calls=%async_computation.2 | async-start | bytes 262144 | tf_op jit(solution)/shard_map/all_to_all | solution.py:76
  129.3 10.0 %all-to-all-done.2 = f32[2,128,6]{2,0,1:T(2,128)S(1)} async-done(((f32[2,128,6]{2,0,1:T(2,128)}), f32[2,128,6]{2,0,1:T(2,128)S(1)}, u32[]{:S(2)}, u32[]{:S(2)}) %all-to-all-start.2) | async-done | bytes 6176 | tf_op jit(solution)/shard_map/all_to_all | solution.py:76
  139.2 0.2 reshape.83
  139.4 6.1 %gather_fusion = f32[768]{0:T(1024)} fusion(f32[1536]{0:T(1024)S(1)} %reshape.83, s32[1024]{0:T(1024)S(1)} %pad_clamp_fusion), kind=kCustom, calls=%fused_computation | custom fusion | bytes 9216 | tf_op jit(solution)/shard_map/gather | solution.py:83
  (28 shorter events, 0.5 us)
Async XLA Ops:
  0.8 16.7 %copy-start = (bf16[768,1024]{1,0:T(8,128)(2,1)S(1)}, bf16[768,1024]{1,0:T(8,128)(2,1)}, u32[]{:S(2)}) copy-start(bf16[768,1024]{1,0:T(8,128)(2,1)} %param.5) | copy-start | bytes 4718596
  6.0 35.6 %all-to-all-start = ((s32[128,2,1,6]{3,1,2,0:T(2,128)}), s32[128,2,1,6]{3,1,2,0:T(2,128)S(1)}, u32[]{:S(2)}, u32[]{:S(2)}) async-start(s32[128,2,1,6]{3,1,2,0:T(2,128)} %bitcast.4), calls=%async_computation | async-start | bytes 262144 | tf_op jit(solution)/shard_map/all_to_all | solution.py:65
  41.6 51.8 %all-to-all-start.1 = ((bf16[128,2,1,6,1024]{4,1,3,2,0:T(2,128)(2,1)}), bf16[128,2,1,6,1024]{4,1,3,2,0:T(2,128)(2,1)S(1)}, u32[]{:S(2)}, u32[]{:S(2)}) async-start(bf16[128,2,1,6,1024]{4,1,3,2,0:T(2,128)(2,1)} %copy.14), calls=%async_computation.1 | async-start | bytes 6291456 | tf_op jit(solution)/shard_map/all_to_all | solution.py:58
  125.4 13.8 %all-to-all-start.2 = ((f32[2,128,6]{2,0,1:T(2,128)}), f32[2,128,6]{2,0,1:T(2,128)S(1)}, u32[]{:S(2)}, u32[]{:S(2)}) async-start(f32[2,128,6]{2,0,1:T(2,128)} %copy.16), calls=%async_computation.2 | async-start | bytes 262144 | tf_op jit(solution)/shard_map/all_to_all | solution.py:76
where the time goes:
time: 146 us
  waiting for transfers between devices  51.9 us (36%)
  local copies, waits for them, and re-layouts  31.3 us (21%)
  starting transfers between devices  25.1 us (17%)
  matrix products  13.9 us (10%)
  other arithmetic  13.1 us (9%)
  loops' own time  10.2 us (7%)
    all_to_all x1, waiting for transfers between devices, local(): lax.all_to_all(outgoing.reshape(devices, SUB, 1, per_label, width), ('sha...  41.9 us
    dot_general x6, matrix products, one_tile(): lax.dot_general(block, members, (((1,), (1,)), ((), ())), preferred_eleme...  13.9 us
    reshape x2, local copies, waits for them, and re-layouts, local(): outgoing.reshape(devices, SUB, 1, per_label, width)  13.1 us
    all_to_all x1, starting transfers between devices, local(): lax.all_to_all(out_fill.reshape(devices, SUB, 1, per_label), ('shard', 'g...  11.5 us
    scatter x1, other arithmetic, local(): jnp.zeros((devices * SUB * per_label, width), jnp.bfloat16).at[slot_index]  10.6 us
    another operation x1, loops' own time, score_full(): lax.map(one_tile, jnp.arange(group_count * tile_count, dtype=jnp.int32))  10.2 us
    all_to_all x1, waiting for transfers between devices, local(): lax.all_to_all(best_score.reshape(SUB, devices, per_label), ('shard', 'gr...  9.98 us
    all_to_all x1, starting transfers between devices, local(): lax.all_to_all(outgoing.reshape(devices, SUB, 1, per_label, width), ('sha...  9.76 us
  transfers between devices with their start and end apart: 3, of which 2 were waited for; matrix products, arithmetic and copies ran while one was open for 17% of the time, Pallas kernels for 0%

commit v1 on v0

v1 whole, which is shorter than its diff:
```python
import jax
import jax.numpy as jnp
from jax import lax
from jax.experimental import pallas as pl
from jax.experimental.pallas import tpu as pltpu
from jax.sharding import PartitionSpec as P

SUB = 2
AXES = ("shard", "grp")
PER_LABEL = 6
WHOLE = 4
BLOCK = 256
MARK = 2.0
BF16 = jnp.bfloat16
F32 = jnp.float32


def one_hot(flags):
    return jnp.where(flags, 1.0, 0.0).astype(BF16)


def dot(a, b):
    return jnp.dot(a, b, preferred_element_type=F32)


def iota(shape, dim):
    return lax.broadcasted_iota(jnp.int32, shape, dim)


def pack_kernel(worker_ref, label_ref, emb_ref, out_ref, slot_ref):
    rows, width = emb_ref.shape
    half = width // 2
    devices = out_ref.shape[0] // 8
    clusters = devices * SUB
    worker = worker_ref[...]
    label = label_ref[...]
    cluster = worker * SUB + label

    member = iota((clusters, rows), 0) == cluster
    member_hot = one_hot(member)
    before = one_hot(iota((rows, rows), 0) < iota((rows, rows), 1))
    earlier = dot(member_hot, before)
    rank = jnp.sum(jnp.where(member, earlier, 0.0), axis=0, keepdims=True).astype(jnp.int32)
    slot_ref[...] = label * PER_LABEL + rank
    first = worker * 8 + label * 4
    whole_row = jnp.where(rank < WHOLE, first + rank, -1)
    half_row = jnp.where(rank < WHOLE, -2, first + (rank - WHOLE) * 2)
    total = dot(member_hot, jnp.ones((rows, 128), BF16)).astype(BF16)

    values = emb_ref[...].astype(F32)
    unit = (values * lax.rsqrt(jnp.sum(values * values, axis=1, keepdims=True) + 1e-06)).astype(BF16)
    left, right = unit[:, :half], unit[:, half:]

    spread = one_hot(iota((BLOCK, BLOCK // 4), 0) // 4 == iota((BLOCK, BLOCK // 4), 1))
    lane = iota((BLOCK, 128), 1)
    place = iota((BLOCK, 128), 0) % 4
    for block in range(devices * 8 // BLOCK):
        at = pl.ds(block * BLOCK, BLOCK)
        here = iota((BLOCK, rows), 0) + block * BLOCK
        count = dot(spread, total[block * BLOCK // 4 : (block + 1) * BLOCK // 4])
        held = dot(one_hot(here == whole_row), unit)
        empty = jnp.where((lane == 0) & (count <= place.astype(F32)), MARK, 0.0)
        out_ref[at, :128] = (held[:, :128] + empty).astype(BF16)
        out_ref[at, 128:width] = held[:, 128:].astype(BF16)
        held = dot(one_hot(here == half_row), left) + dot(one_hot(here == half_row + 1), right)
        empty = (lane == 0) & (place % 2 == 0) & (count <= (WHOLE + place // 2).astype(F32))
        empty = jnp.where(empty, MARK, 0.0)
        out_ref[at, width : width + 128] = (held[:, :128] + empty).astype(BF16)
        out_ref[at, width + 128 :] = held[:, 128:].astype(BF16)


def score_kernel(in_ref, best_ref, members):
    rows = in_ref.shape[0]
    devices = rows // 8
    width = members.shape[2]
    half = width // 2
    per_block = BLOCK // 8
    r, c = iota((BLOCK, BLOCK), 0), iota((BLOCK, BLOCK), 1)
    regroup = one_hot(c == r % per_block * 8 + r // per_block)
    for block in range(rows // BLOCK):
        at = pl.ds(block * BLOCK, BLOCK)
        whole = dot(regroup, in_ref[at, :width]).astype(BF16)
        halves = dot(regroup, in_ref[at, width:]).astype(BF16)
        for sub in range(8):
            lab, j = sub // 4, sub % 4
            piece = slice(sub * per_block, (sub + 1) * per_block)
            members[lab, pl.ds(j * devices + block * per_block, per_block), :] = whole[piece]
            to = pl.ds((WHOLE + j // 2) * devices + block * per_block, per_block)
            members[lab, to, pl.ds(j % 2 * half, half)] = halves[piece]
    count = members.shape[1]
    eye = jnp.where(iota((BLOCK, BLOCK), 0) == iota((BLOCK, BLOCK), 1), -8.0, 0.0)
    found = []
    for lab in range(SUB):
        everyone = members[lab]
        best = jnp.full((1, count), -8.0, F32)
        for block in range(count // BLOCK):
            at = slice(block * BLOCK, (block + 1) * BLOCK)
            mine = everyone[at]
            scores = lax.dot_general(
                mine, everyone, (((1,), (1,)), ((), ())), preferred_element_type=F32
            )
            absent = jnp.where(mine[:, :1].astype(F32) > 1.5, -8.0, 0.0)
            scores = scores + absent
            parts = []
            for other in range(count // BLOCK):
                part = scores[:, other * BLOCK : (other + 1) * BLOCK]
                if other == block:
                    part = part + eye
                parts.append(jnp.max(part, axis=0, keepdims=True))
            best = jnp.maximum(best, jnp.concatenate(parts, axis=1))
        best = jnp.where(best < -2.0, -1.0, best)
        found += [best[:, j * devices : (j + 1) * devices] for j in range(PER_LABEL)]
    found.append(jnp.zeros((128 - SUB * PER_LABEL, devices), F32))
    best_ref[...] = jnp.concatenate(found, axis=0).T


def unpack_kernel(worker_ref, slot_ref, back_ref, out_ref):
    rows = worker_ref.shape[1]
    back = back_ref[...]
    devices = back.shape[0]
    back = back.T[:16]
    high = back.astype(BF16)
    rest = back - high.astype(F32)
    middle = rest.astype(BF16)
    low = (rest - middle.astype(F32)).astype(BF16)
    chosen = one_hot(iota((devices, rows), 0) == worker_ref[...])
    values = dot(high, chosen) + dot(middle, chosen) + dot(low, chosen)
    mine = iota((16, rows), 0) == slot_ref[...]
    out_ref[...] = jnp.sum(jnp.where(mine, values, 0.0), axis=0, keepdims=True)


VMEM = pl.BlockSpec(memory_space=pltpu.VMEM)


def local(embeddings, worker, label):
    rows, width = embeddings.shape
    devices = lax.axis_size("shard") * lax.axis_size("grp")
    params = pltpu.CompilerParams(vmem_limit_bytes=40 * 2**20)
    worker = worker.reshape(1, rows)
    label = label.reshape(1, rows)
    outgoing, slot = pl.pallas_call(
        pack_kernel,
        out_shape=(
            jax.ShapeDtypeStruct((devices * 8, width * 3 // 2), BF16),
            jax.ShapeDtypeStruct((1, rows), jnp.int32),
        ),
        in_specs=[VMEM] * 3,
        out_specs=(VMEM, VMEM),
        compiler_params=params,
        name="pack",
    )(worker, label, embeddings)
    incoming = lax.all_to_all(
        outgoing.reshape(devices, 8, width * 3 // 2), AXES, split_axis=0, concat_axis=0, tiled=True
    )
    best = pl.pallas_call(
        score_kernel,
        out_shape=jax.ShapeDtypeStruct((devices, 128), F32),
        in_specs=[VMEM],
        out_specs=VMEM,
        scratch_shapes=[pltpu.VMEM((SUB, devices * PER_LABEL, width), BF16)],
        compiler_params=params,
        name="score",
    )(incoming.reshape(devices * 8, width * 3 // 2))
    returned = lax.all_to_all(
        best.reshape(devices, 1, 128), AXES, split_axis=0, concat_axis=0, tiled=True
    )
    nearest = pl.pallas_call(
        unpack_kernel,
        out_shape=jax.ShapeDtypeStruct((1, rows), F32),
        in_specs=[VMEM] * 3,
        out_specs=VMEM,
        compiler_params=params,
        name="unpack",
    )(worker, slot, returned.reshape(devices, 128))
    return nearest.reshape(rows)


def solution(mesh):
    return jax.shard_map(
        local,
        mesh=mesh,
        in_specs=(P(AXES, None), P(AXES), P(AXES)),
        out_specs=P(AXES),
        check_vma=False,
    )
```

time: 146 us -> 78.1 us (0.53)
  blocking collectives: 0 us -> 66.4 us
  waiting for transfers between devices: 51.9 us -> 0 us
  local copies, waits for them, and re-layouts: 31.3 us -> 2.79 us
  starting transfers between devices: 25.1 us -> 0 us
  matrix products: 13.9 us -> 0 us
  other arithmetic: 13.1 us -> 0.61 us
  loops' own time: 10.2 us -> 0 us
  Pallas kernels: 0 us -> 8.08 us
    all_to_all x0 -> x2, blocking collectives: none -> 66.4 us  [the longest x1 53.4 us: local(): lax.all_to_all(outgoing.reshape(devices, 8, width * 3 // 2), AXES, split_...]
    all_to_all x3 -> x0, waiting for transfers between devices: 51.9 us -> none  [the longest x1 41.9 us: local(): lax.all_to_all(outgoing.reshape(devices, SUB, 1, per_label, width), ('sha...]
    all_to_all x3 -> x0, starting transfers between devices: 25.1 us -> none  [the longest x1 11.5 us: local(): lax.all_to_all(out_fill.reshape(devices, SUB, 1, per_label), ('shard', 'g...]
    dot_general x6 -> x0, matrix products: 13.9 us -> none  [one_tile(): lax.dot_general(block, members, (((1,), (1,)), ((), ())), preferred_eleme...]
    reshape x6 -> x2, local copies, waits for them, and re-layouts: 14.4 us -> 1.38 us  [the longest x1 0.69 us: local(): label = label.reshape(1, rows)]
    scatter x1 -> x0, other arithmetic: 10.6 us -> none  [local(): jnp.zeros((devices * SUB * per_label, width), jnp.bfloat16).at[slot_index]]
    another operation x1 -> x0, loops' own time: 10.2 us -> none  [score_full(): lax.map(one_tile, jnp.arange(group_count * tile_count, dtype=jnp.int32))]
    pallas_call x0 -> x3, Pallas kernels: none -> 8.08 us  [the longest x1 4.27 us: local(): pl.pallas_call(pack_kernel, out_shape=(jax.ShapeDtypeStruct((devices * 8,...]
  transfers between devices with their start and end apart: 3 -> 0, of which waited for: 2 -> 0; matrix products, arithmetic and copies ran while one was open for 17% -> 0% of each run, Pallas kernels for 0% -> 0%
where the time goes in v1:
time: 78.1 us; the launch traced here: 77.9 us
  blocking collectives  66.4 us (85%)
  Pallas kernels  8.08 us (10%)
  local copies, waits for them, and re-layouts  2.79 us (4%)
    all_to_all x1, blocking collectives, local(): lax.all_to_all(outgoing.reshape(devices, 8, width * 3 // 2), AXES, split_...  53.4 us
    all_to_all x1, blocking collectives, local(): lax.all_to_all(best.reshape(devices, 1, 128), AXES, split_axis=0, concat_...  13 us
    pallas_call x1, Pallas kernels, local(): pl.pallas_call(pack_kernel, out_shape=(jax.ShapeDtypeStruct((devices * 8,...  4.27 us
    pallas_call x1, Pallas kernels, local(): pl.pallas_call(score_kernel, out_shape=jax.ShapeDtypeStruct((devices, 128...  3.54 us

profile of v1, /device:TPU:1, one launch (start us, length us, event | category | flops | bytes accessed | tf_op | source)
XLA Modules:
  0.0 77.9 jit_solution(5201786425994714309)
XLA Ops:
  0.0 0.7 reshape.21.worker_ref
  0.7 0.7 reshape.22.label_ref
  1.4 0.0 copy-start
  1.4 1.4 %copy-done = bf16[768,1024]{1,0:T(8,128)(2,1)S(1)} copy-done((bf16[768,1024]{1,0:T(8,128)(2,1)S(1)}, bf16[768,1024]{1,0:T(8,128)(2,1)}, u32[]{:S(2)}) %copy-start) | copy-done | bytes 1572888
  2.8 4.3 %pack.1 = (bf16[1024,1536]{1,0:T(8,128)(2,1)S(1)}, s32[1,768]{1,0:T(1,128)S(1)}) custom-call(s32[1,768]{1,0:T(1,128)S(1)} %reshape.21.worker_ref, s32[1,768]{1,0:T(1,128)S(1)} %reshape.22.label_ref, bf16[768,1024]{1,0:T(8,128)(2,1)S(1)} %copy-done), custom_call_target="tpu_custom_call" | custom-call | tf_op jit(solution)/shard_map/pack/pallas_call | solution.py:141
  7.1 53.4 %all_to_all.10 = bf16[128,8,1536]{2,1,0:T(8,128)(2,1)S(1)} all-to-all(bf16[128,8,1536]{2,1,0:T(8,128)(2,1)S(1)} %bitcast.7), channel_id=1, replica_groups=mesh['shard'=32,'grp'=4] {'shard','grp'}, dimensions={0} | all-to-all | bytes 6291456 | tf_op jit(solution)/shard_map/all_to_all | solution.py:152
  60.4 3.5 %score.1 = f32[128,128]{1,0:T(8,128)S(1)} custom-call(bf16[1024,1536]{1,0:T(8,128)(2,1)S(1)} %bitcast.6), custom_call_target="tpu_custom_call" | custom-call | tf_op jit(solution)/shard_map/score/pallas_call | solution.py:155
  64.0 13.0 %all_to_all.11 = f32[128,1,128]{2,1,0:T(1,128)S(1)} all-to-all(f32[128,1,128]{2,1,0:T(1,128)S(1)} %bitcast.8), channel_id=1, replica_groups=mesh['shard'=32,'grp'=4] {'shard','grp'}, dimensions={0} | all-to-all | bytes 131072 | tf_op jit(solution)/shard_map/all_to_all | solution.py:164
  77.0 0.3 unpack.1
  77.2 0.6 reduce
Async XLA Ops:
  1.4 1.4 %copy-start = (bf16[768,1024]{1,0:T(8,128)(2,1)S(1)}, bf16[768,1024]{1,0:T(8,128)(2,1)}, u32[]{:S(2)}) copy-start(bf16[768,1024]{1,0:T(8,128)(2,1)} %emb_ref.1) | copy-start | bytes 4718596

commit v2 on v1

v2 whole, which is shorter than its diff:
```python
import functools

import jax
import jax.numpy as jnp
from jax import lax
from jax.experimental import pallas as pl
from jax.experimental.pallas import tpu as pltpu
from jax.sharding import PartitionSpec as P

SUB = 2
AXES = ("shard", "grp")
PER_LABEL = 6
WHOLE = 4
LATE = 2
BLOCK = 256
MARK = 2.0
BF16 = jnp.bfloat16
F32 = jnp.float32


def one_hot(flags):
    return jnp.where(flags, 1.0, 0.0).astype(BF16)


def dot(a, b):
    return jnp.dot(a, b, preferred_element_type=F32)


def dot_rows(a, b):
    return lax.dot_general(a, b, (((1,), (1,)), ((), ())), preferred_element_type=F32)


def iota(shape, dim):
    return lax.broadcasted_iota(jnp.int32, shape, dim)


def pack_kernel(worker_hbm, label_hbm, emb_hbm, out_ref, place_ref, worker_ref, label_ref, emb, late, arrived):
    rows, width = emb.shape
    half = width // 2
    clusters = out_ref.shape[0] // 4
    fetches = [
        pltpu.make_async_copy(worker_hbm, worker_ref, arrived.at[0]),
        pltpu.make_async_copy(label_hbm, label_ref, arrived.at[1]),
        pltpu.make_async_copy(emb_hbm, emb, arrived.at[2]),
    ]
    for fetch in fetches:
        fetch.start()
    before = one_hot(iota((rows, rows), 0) < iota((rows, rows), 1))
    fetches[0].wait()
    fetches[1].wait()
    worker = worker_ref[...].reshape(1, rows)
    label = label_ref[...].reshape(1, rows)
    cluster = worker * SUB + label

    member = iota((clusters, rows), 0) == cluster
    member_hot = one_hot(member)
    earlier = dot(member_hot, before)
    rank = jnp.sum(jnp.where(member, earlier, 0.0), axis=0, keepdims=True).astype(jnp.int32)
    place_ref[...] = worker * 16 + label * PER_LABEL + rank
    whole_row = jnp.where(rank < WHOLE, cluster * WHOLE + rank, -1)
    late_row = jnp.where(rank < WHOLE, -1, cluster * LATE + rank - WHOLE)
    total = dot(member_hot, jnp.ones((rows, 128), BF16)).astype(BF16)
    line = iota((BLOCK, rows), 0).astype(F32).astype(BF16)
    fetches[2].wait()

    def placed(block, target, per_cluster, first_slot, to):
        at = pl.ds(block * BLOCK, BLOCK)
        count = BLOCK // per_cluster
        inside = target - block * BLOCK
        inside = jnp.where((inside >= 0) & (inside < BLOCK), inside, -1).astype(F32).astype(BF16)
        chosen = jnp.where(line == inside, jnp.ones((), BF16), jnp.zeros((), BF16))
        values = dot(chosen, emb[...])
        values = values * lax.rsqrt(jnp.sum(values * values, axis=1, keepdims=True) + 1e-06)
        spread = one_hot(iota((BLOCK, count), 0) // per_cluster == iota((BLOCK, count), 1))
        filled = dot(spread, total[block * count : (block + 1) * count])
        slot = iota((BLOCK, 128), 0) % per_cluster + first_slot
        empty = (iota((BLOCK, 128), 1) == 0) & (filled <= slot.astype(F32))
        to[at, :128] = (values[:, :128] + jnp.where(empty, MARK, 0.0)).astype(BF16)
        to[at, 128:width] = values[:, 128:].astype(BF16)

    for block in range(clusters * LATE // BLOCK):
        placed(block, late_row, LATE, WHOLE, late)
    for block in range(clusters * WHOLE // BLOCK):
        placed(block, whole_row, WHOLE, 0, out_ref)
    r, c = iota((BLOCK, BLOCK), 0), iota((BLOCK, BLOCK), 1)
    split = one_hot(c == r % 2 * (BLOCK // 2) + r // 2)
    for block in range(clusters * LATE * 2 // BLOCK):
        source = pl.ds(block * (BLOCK // 2), BLOCK // 2)
        halves = jnp.concatenate([late[source, :half], late[source, half:]], axis=0)
        out_ref[pl.ds(block * BLOCK, BLOCK), width:] = dot(split, halves).astype(BF16)


def score_kernel(in_ref, out_ref, members):
    rows = in_ref.shape[0]
    devices = rows // 8
    count, width = members.shape[1:]
    half = width // 2
    per_block = BLOCK // 8
    r, c = iota((BLOCK, BLOCK), 0), iota((BLOCK, BLOCK), 1)
    regroup = one_hot(c == r % per_block * 8 + r // per_block)
    itself = jnp.where(r == c, -8.0, 0.0)
    for block in range(rows // BLOCK):
        at = pl.ds(block * BLOCK, BLOCK)
        whole = dot(regroup, in_ref[at, :width]).astype(BF16)
        halves = dot(regroup, in_ref[at, width:]).astype(BF16)
        for sub in range(8):
            lab, j = sub // 4, sub % 4
            piece = slice(sub * per_block, (sub + 1) * per_block)
            members[lab, pl.ds(j * devices + block * per_block, per_block), :] = whole[piece]
            to = pl.ds((WHOLE + j // 2) * devices + block * per_block, per_block)
            members[lab, to, pl.ds(j % 2 * half, half)] = halves[piece]

    blocks = count // BLOCK
    found = []
    for lab in range(SUB):
        parts = [members[lab, pl.ds(i * BLOCK, BLOCK), :] for i in range(blocks)]
        absent = [jnp.where(p[:, :128].astype(F32) > MARK - 0.5, -8.0, 0.0)[:, :1] for p in parts]
        absent_row = [jnp.broadcast_to(a, (BLOCK, 128)).T[:1] for a in absent]
        down, along = [[] for _ in parts], [[] for _ in parts]
        for i in range(blocks):
            for j in range(i, blocks):
                scores = dot_rows(parts[i], parts[j]) + absent[i]
                if i == j:
                    down[j].append(scores + itself)
                else:
                    down[j].append(scores)
                    scores = scores + absent_row[j]
                    along[i] += [scores[:, k : k + 128] for k in range(0, BLOCK, 128)]
        for i in range(blocks):
            best = jnp.max(functools.reduce(jnp.maximum, down[i]), axis=0, keepdims=True)
            if along[i]:
                other = functools.reduce(jnp.maximum, along[i]).T
                best = jnp.maximum(best, jnp.max(other, axis=0, keepdims=True))
            best = jnp.where(best < -2.0, -1.0, best)
            found += [best[:, k : k + devices] for k in range(0, BLOCK, devices)]
    found.append(jnp.zeros((128 - SUB * PER_LABEL, devices), F32))
    out_ref[...] = jnp.concatenate(found, axis=0).T


def unpack_kernel(place_ref, back_ref, out_ref):
    place = place_ref[...]
    rows = place.shape[1]
    back = back_ref[...]
    devices = back.shape[0]
    back = back.T[:16]
    high = back.astype(BF16)
    rest = back - high.astype(F32)
    middle = rest.astype(BF16)
    low = (rest - middle.astype(F32)).astype(BF16)
    chosen = one_hot(iota((devices, rows), 0) == place // 16)
    values = dot(high, chosen) + dot(middle, chosen) + dot(low, chosen)
    mine = iota((16, rows), 0) == place % 16
    out_ref[...] = jnp.sum(jnp.where(mine, values, 0.0), axis=0)


VMEM = pl.BlockSpec(memory_space=pltpu.VMEM)
HBM = pl.BlockSpec(memory_space=pltpu.HBM)
PARAMS = pltpu.CompilerParams(vmem_limit_bytes=40 * 2**20)


def exchange(array):
    return lax.all_to_all(array, AXES, split_axis=0, concat_axis=0, tiled=True)


def local(embeddings, worker, label):
    rows, width = embeddings.shape
    devices = lax.axis_size("shard") * lax.axis_size("grp")
    shape = jax.ShapeDtypeStruct
    packed = (devices * 8, width * 3 // 2)
    in_hbm = [pltpu.with_memory_space_constraint(x, pltpu.HBM) for x in (worker, label, embeddings)]
    outgoing, place = pl.pallas_call(
        pack_kernel,
        out_shape=(shape(packed, BF16), shape((1, rows), jnp.int32)),
        in_specs=[HBM] * 3,
        out_specs=(VMEM, VMEM),
        scratch_shapes=[
            pltpu.VMEM((rows,), jnp.int32),
            pltpu.VMEM((rows,), jnp.int32),
            pltpu.VMEM((rows, width), BF16),
            pltpu.VMEM((devices * SUB * LATE, width), BF16),
            pltpu.SemaphoreType.DMA((3,)),
        ],
        compiler_params=PARAMS,
        name="pack",
    )(*in_hbm)
    incoming = exchange(outgoing.reshape(devices, 8, packed[1])).reshape(packed)
    found = pl.pallas_call(
        score_kernel,
        out_shape=shape((devices, 128), F32),
        in_specs=[VMEM],
        out_specs=VMEM,
        scratch_shapes=[pltpu.VMEM((SUB, devices * PER_LABEL, width), BF16)],
        compiler_params=PARAMS,
        name="score",
    )(incoming)
    returned = exchange(found.reshape(devices, 1, 128)).reshape(devices, 128)
    return pl.pallas_call(
        unpack_kernel,
        out_shape=shape((rows,), F32),
        in_specs=[VMEM] * 2,
        out_specs=VMEM,
        compiler_params=PARAMS,
        name="unpack",
    )(place, returned)


def solution(mesh):
    return jax.shard_map(
        local,
        mesh=mesh,
        in_specs=(P(AXES, None), P(AXES), P(AXES)),
        out_specs=P(AXES),
        check_vma=False,
    )
```

time: 78.1 us -> 74.8 us (0.958)
  local copies, waits for them, and re-layouts: 2.79 us -> 0 us
    unnamed x2 -> x0, local copies, waits for them, and re-layouts: 1.41 us -> none
    reshape x2 -> x0, local copies, waits for them, and re-layouts: 1.38 us -> none  [the longest x1 0.69 us: local(): label = label.reshape(1, rows)]
where the time goes in v2:
time: 74.8 us; the launch traced here: 74.6 us
  blocking collectives  66.4 us (89%)
  Pallas kernels  8.22 us (11%)
    all_to_all x2, blocking collectives, exchange(): return lax.all_to_all(array, AXES, split_axis=0, concat_axis=0, tiled=True)  66.4 us
    pallas_call x1, Pallas kernels, local(): pl.pallas_call(pack_kernel, out_shape=(shape(packed, BF16), shape((1, row...  4.56 us
    pallas_call x1, Pallas kernels, local(): pl.pallas_call(score_kernel, out_shape=shape((devices, 128), F32), in_spe...  2.8 us

profile of v2, /device:TPU:1, one launch (start us, length us, event | category | flops | bytes accessed | tf_op | source)
XLA Modules:
  0.0 74.6 jit_solution(4505102397995315795)
XLA Ops:
  0.0 4.6 %pack.1 = (bf16[1024,1536]{1,0:T(8,128)(2,1)S(1)}, s32[1,768]{1,0:T(1,128)S(1)}) custom-call(s32[768]{0:T(1024)} %worker_hbm.1, s32[768]{0:T(1024)} %label_hbm.1, bf16[768,1024]{1,0:T(8,128)(2,1)} %emb_hbm.1), custom_call_target="tpu_custom_call" | custom-call | tf_op jit(solution)/shard_map/pack/pallas_call | solution.py:171
  4.6 53.4 %all_to_all.10 = bf16[128,8,1536]{2,1,0:T(8,128)(2,1)S(1)} all-to-all(bf16[128,8,1536]{2,1,0:T(8,128)(2,1)S(1)} %bitcast.7), channel_id=1, replica_groups=mesh['shard'=32,'grp'=4] {'shard','grp'}, dimensions={0} | all-to-all | bytes 6291456 | tf_op jit(solution)/shard_map/all_to_all | solution.py:162
  57.9 2.8 %score.1 = f32[128,128]{1,0:T(8,128)S(1)} custom-call(bf16[1024,1536]{1,0:T(8,128)(2,1)S(1)} %bitcast.6), custom_call_target="tpu_custom_call" | custom-call | tf_op jit(solution)/shard_map/score/pallas_call | solution.py:187
  60.7 13.0 %all_to_all.11 = f32[128,1,128]{2,1,0:T(1,128)S(1)} all-to-all(f32[128,1,128]{2,1,0:T(1,128)S(1)} %bitcast.8), channel_id=1, replica_groups=mesh['shard'=32,'grp'=4] {'shard','grp'}, dimensions={0} | all-to-all | bytes 131072 | tf_op jit(solution)/shard_map/all_to_all | solution.py:162
  73.7 0.9 %unpack.1 = f32[768]{0:T(1024)} custom-call(s32[1,768]{1,0:T(1,128)S(1)} %get-tuple-element.7.place_ref, f32[128,128]{1,0:T(8,128)S(1)} %bitcast.9), custom_call_target="tpu_custom_call" | custom-call | tf_op jit(solution)/shard_map/unpack/pallas_call | solution.py:197

commit v3 on v2

v3 whole, which is shorter than its diff:
```python
import functools

import jax
import jax.numpy as jnp
from jax import lax
from jax.experimental import pallas as pl
from jax.experimental.pallas import tpu as pltpu
from jax.sharding import PartitionSpec as P

SUB = 2
AXES = ("shard", "grp")
PER_LABEL = 6
WHOLE = 4
LATE = 2
BLOCK = 256
MARK = 2.0
BF16 = jnp.bfloat16
F32 = jnp.float32


def one_hot(flags):
    return jnp.where(flags, 1.0, 0.0).astype(BF16)


def dot(a, b):
    return jnp.dot(a, b, preferred_element_type=F32)


def dot_rows(a, b):
    return lax.dot_general(a, b, (((1,), (1,)), ((), ())), preferred_element_type=F32)


def iota(shape, dim):
    return lax.broadcasted_iota(jnp.int32, shape, dim)


def small(index):
    return index.astype(F32).astype(BF16)


def merged_rows(a, b, part, swap=0):
    rows, width = a.shape
    first = small((iota((1, 16, width), 1) ^ swap * part) & (2 * part - 1)) < part
    a, b = a.reshape(rows // 16, 16, width), b.reshape(rows // 16, 16, width)
    return jnp.where(first, a, b).reshape(rows, width)


def turned(x):
    rows, width = x.shape
    return pltpu.roll(x.reshape(rows // 8, 8, width), 4, 1).reshape(rows, width)


def upper_half():
    return (lax.axis_index(AXES) >= lax.axis_size(AXES) // 2).astype(jnp.int32)


def pack_kernel(worker_hbm, label_hbm, emb_hbm, out_ref, place_ref, worker_ref, label_ref, emb, arrived):
    rows, width = emb.shape
    half = width // 2
    clusters = out_ref.shape[0] // 4
    pairs = clusters // 4
    fetches = [
        pltpu.make_async_copy(worker_hbm, worker_ref, arrived.at[0]),
        pltpu.make_async_copy(label_hbm, label_ref, arrived.at[1]),
        pltpu.make_async_copy(emb_hbm, emb, arrived.at[2]),
    ]
    for fetch in fetches:
        fetch.start()
    before = one_hot(iota((BLOCK, BLOCK), 0) < iota((BLOCK, BLOCK), 1))
    ones = jnp.ones((BLOCK, 128), BF16)
    line = small(iota((BLOCK, rows), 0))
    first_lane = iota((BLOCK, 128), 1) == 0
    fetches[0].wait()
    fetches[1].wait()
    worker = worker_ref[...].reshape(1, rows)
    label = label_ref[...].reshape(1, rows)
    side = label ^ upper_half()
    cluster = worker * SUB + side

    member = iota((clusters, rows), 0) == cluster
    member_hot = one_hot(member)
    count = jnp.zeros((clusters, 128), F32)
    earlier = []
    for part in range(0, rows, BLOCK):
        these = member_hot[:, part : part + BLOCK]
        inside = dot(these, before)
        earlier += [inside[:, k : k + 128] + count for k in range(0, BLOCK, 128)]
        count = count + dot(these, ones)
    earlier = jnp.concatenate(earlier, axis=1)
    rank = jnp.sum(jnp.where(member, earlier, 0.0), axis=0, keepdims=True).astype(jnp.int32)
    place_ref[...] = worker * 16 + label * PER_LABEL + rank
    total = count.astype(BF16)
    whole_row = jnp.where(rank < WHOLE, cluster * WHOLE + rank, -1)
    late_row = (worker & (pairs - 1)) * 8 + side * LATE + rank - WHOLE
    upper = (worker >= pairs).astype(jnp.int32)
    left_row = jnp.where(rank < WHOLE, -1, late_row + upper * 4)
    right_row = jnp.where(rank < WHOLE, -1, late_row + (1 - upper) * 4)
    fetches[2].wait()

    def chosen(block, target):
        inside = target - block * BLOCK
        inside = jnp.where((inside >= 0) & (inside < BLOCK), inside, -1)
        return jnp.where(line == small(inside), jnp.ones((), BF16), jnp.zeros((), BF16))

    def empty(spread, counts, slot):
        return jnp.where(first_lane & (dot(one_hot(spread), counts) <= slot.astype(F32)), MARK, 0.0)

    r, c = iota((BLOCK, 128), 0), iota((BLOCK, 128), 1)
    for block in range(pairs * 8 // BLOCK):
        left = dot(chosen(block, left_row), emb[:, :half])
        right = dot(chosen(block, right_row), emb[:, half:])
        left_sum = jnp.broadcast_to(jnp.sum(left * left, axis=1, keepdims=True), (BLOCK, 128))
        right_sum = jnp.broadcast_to(jnp.sum(right * right, axis=1, keepdims=True), (BLOCK, 128))
        left_scale = lax.rsqrt(left_sum + turned(right_sum) + 1e-06)[:, :1]
        right_scale = lax.rsqrt(right_sum + turned(left_sum) + 1e-06)[:, :1]
        per_block = BLOCK // 8 * SUB
        counts = [total[at + block * per_block :][:per_block] for at in (0, clusters // 2)]
        spread = c == (r >> 2 & 1) * per_block + (r >> 3) * SUB + (r >> 1 & 1)
        mark = empty(spread, jnp.concatenate(counts, axis=0), WHOLE + (r & 1))
        left = left * left_scale
        left = jnp.concatenate([left[:, :128] + mark, left[:, 128:]], axis=1).astype(BF16)
        right = (right * right_scale).astype(BF16)
        out_ref[pl.ds(block * BLOCK, BLOCK), width:] = merged_rows(left, right, 4)
        out_ref[pl.ds((block + pairs * 8 // BLOCK) * BLOCK, BLOCK), width:] = merged_rows(right, left, 4)
    r, c = iota((BLOCK, BLOCK // WHOLE), 0), iota((BLOCK, BLOCK // WHOLE), 1)
    for block in range(clusters * WHOLE // BLOCK):
        at = pl.ds(block * BLOCK, BLOCK)
        values = dot(chosen(block, whole_row), emb[...])
        values = values * lax.rsqrt(jnp.sum(values * values, axis=1, keepdims=True) + 1e-06)
        counts = total[block * BLOCK // WHOLE :][: BLOCK // WHOLE]
        mark = empty(c == r >> 2, counts, (iota((BLOCK, 128), 0) & 3))
        out_ref[at, :128] = (values[:, :128] + mark).astype(BF16)
        out_ref[at, 128:width] = values[:, 128:].astype(BF16)


def score_kernel(in_ref, out_ref, members):
    rows = in_ref.shape[0]
    devices = rows // 8
    count, width = members.shape[1:]
    half = width // 2
    wholes = devices * WHOLE

    for at in range(0, wholes, BLOCK):
        lower = in_ref[at : at + BLOCK, :width]
        upper = in_ref[wholes + at : wholes + at + BLOCK, :width]
        members[0, at : at + BLOCK, :] = merged_rows(lower, upper, 4)
        members[1, at : at + BLOCK, :] = merged_rows(upper, lower, 4)
    swap = upper_half()
    lates = wholes // 2
    quarters = [in_ref[k * lates : (k + 1) * lates, width:] for k in range(4)]
    for lab in range(SUB):
        near, far = [
            merged_rows(quarters[k + 2 * lab], quarters[k + 2 - 2 * lab], 2) for k in (0, 1)
        ]
        straight = merged_rows(near, far, 4)
        crossed = turned(merged_rows(far, near, 4).astype(F32)).astype(BF16)
        members[lab, wholes:, :half] = merged_rows(straight, crossed, 4, swap)
        members[lab, wholes:, half:] = merged_rows(crossed, straight, 4, swap)

    r, c = iota((BLOCK, BLOCK), 0), iota((BLOCK, BLOCK), 1)
    itself = jnp.where(r == c, -8.0, 0.0)
    sub, lane = iota((8, 128), 0), iota((8, 128), 1)
    source = (lane & 15) * 8 + sub

    def in_order(best, start, part, owner):
        total = jnp.zeros((8, 128), F32)
        for v in range(part // 16):
            these = jnp.broadcast_to(best[:, start + v * 128 : start + (v + 1) * 128], (8, 128))
            moved = jnp.take_along_axis(these, source, axis=1)
            total = total + jnp.where((lane >> 4) == owner * (part // 16) + v, moved, 0.0)
        return total

    blocks = count // BLOCK
    found = []
    for lab in range(SUB):
        parts = [members[lab, pl.ds(i * BLOCK, BLOCK), :] for i in range(blocks)]
        absent = [jnp.where(p[:, :128].astype(F32) > MARK - 0.5, -8.0, 0.0)[:, :1] for p in parts]
        absent_row = [jnp.broadcast_to(a, (BLOCK, 128)).T[:1] for a in absent]
        down, along = [[] for _ in parts], [[] for _ in parts]
        for i in range(blocks):
            for j in range(i, blocks):
                scores = dot_rows(parts[i], parts[j]) + absent[i]
                if i == j:
                    down[j].append(scores + itself)
                else:
                    down[j].append(scores)
                    scores = scores + absent_row[j]
                    along[i] += [scores[:, k : k + 128] for k in range(0, BLOCK, 128)]
        merged = []
        for i in range(blocks):
            best = jnp.max(functools.reduce(jnp.maximum, down[i]), axis=0, keepdims=True)
            if along[i]:
                other = functools.reduce(jnp.maximum, along[i]).T
                best = jnp.maximum(best, jnp.max(other, axis=0, keepdims=True))
            merged.append(jnp.where(best < -2.0, -1.0, best))
        best = jnp.concatenate(merged, axis=1)
        whole = in_order(best, 0, devices // 2, sub >> 2 ^ lab)
        whole = whole + pltpu.roll(whole, 4, 0)
        late = in_order(best, wholes, devices // 4, (sub >> 2) + ((sub >> 1 & 1) ^ lab) * 2)
        late = late + pltpu.roll(late, 4, 0)
        late = late + pltpu.roll(late, 2, 0)
        found += [whole[:WHOLE], late[:LATE]]
    found.append(jnp.zeros((128 - SUB * PER_LABEL, devices), F32))
    out_ref[...] = jnp.concatenate(found, axis=0).T


def unpack_kernel(place_ref, back_ref, out_ref):
    place = place_ref[...]
    rows = place.shape[1]
    back = back_ref[...]
    devices = back.shape[0]
    back = back.T[:16]
    high = back.astype(BF16)
    rest = back - high.astype(F32)
    middle = rest.astype(BF16)
    low = (rest - middle.astype(F32)).astype(BF16)
    chosen = one_hot(iota((devices, rows), 0) == place >> 4)
    values = dot(high, chosen) + dot(middle, chosen) + dot(low, chosen)
    mine = iota((16, rows), 0) == (place & 15)
    out_ref[...] = jnp.sum(jnp.where(mine, values, 0.0), axis=0)


VMEM = pl.BlockSpec(memory_space=pltpu.VMEM)
HBM = pl.BlockSpec(memory_space=pltpu.HBM)
PARAMS = pltpu.CompilerParams(vmem_limit_bytes=40 * 2**20)


def exchange(array):
    return lax.all_to_all(array, AXES, split_axis=0, concat_axis=0, tiled=True)


def local(embeddings, worker, label):
    rows, width = embeddings.shape
    devices = lax.axis_size("shard") * lax.axis_size("grp")
    shape = jax.ShapeDtypeStruct
    packed = (devices * 8, width * 3 // 2)
    in_hbm = [pltpu.with_memory_space_constraint(x, pltpu.HBM) for x in (worker, label, embeddings)]
    outgoing, place = pl.pallas_call(
        pack_kernel,
        out_shape=(shape(packed, BF16), shape((1, rows), jnp.int32)),
        in_specs=[HBM] * 3,
        out_specs=(VMEM, VMEM),
        scratch_shapes=[
            pltpu.VMEM((rows,), jnp.int32),
            pltpu.VMEM((rows,), jnp.int32),
            pltpu.VMEM((rows, width), BF16),
            pltpu.SemaphoreType.DMA((3,)),
        ],
        compiler_params=PARAMS,
        name="pack",
    )(*in_hbm)
    incoming = exchange(outgoing.reshape(devices, 8, packed[1])).reshape(packed)
    found = pl.pallas_call(
        score_kernel,
        out_shape=shape((devices, 128), F32),
        in_specs=[VMEM],
        out_specs=VMEM,
        scratch_shapes=[pltpu.VMEM((SUB, devices * PER_LABEL, width), BF16)],
        compiler_params=PARAMS,
        name="score",
    )(incoming)
    returned = exchange(found.reshape(devices, 1, 128)).reshape(devices, 128)
    return pl.pallas_call(
        unpack_kernel,
        out_shape=shape((rows,), F32),
        in_specs=[VMEM] * 2,
        out_specs=VMEM,
        compiler_params=PARAMS,
        name="unpack",
    )(place, returned)


def solution(mesh):
    return jax.shard_map(
        local,
        mesh=mesh,
        in_specs=(P(AXES, None), P(AXES), P(AXES)),
        out_specs=P(AXES),
        check_vma=False,
    )
```

time: 74.8 us -> 74 us (0.989)
  Pallas kernels: 8.22 us -> 7.45 us
where the time goes in v3:
time: 74 us; the launch traced here: 73.8 us
  blocking collectives  66.4 us (90%)
  Pallas kernels  7.45 us (10%)
    all_to_all x2, blocking collectives, exchange(): return lax.all_to_all(array, AXES, split_axis=0, concat_axis=0, tiled=True)  66.4 us
    pallas_call x1, Pallas kernels, local(): pl.pallas_call(pack_kernel, out_shape=(shape(packed, BF16), shape((1, row...  4.45 us
    pallas_call x1, Pallas kernels, local(): pl.pallas_call(score_kernel, out_shape=shape((devices, 128), F32), in_spe...  2.14 us

profile of v3, /device:TPU:1, one launch (start us, length us, event | category | flops | bytes accessed | tf_op | source)
XLA Modules:
  0.0 73.8 jit_solution(3354434645648253615)
XLA Ops:
  0.0 4.5 %pack.1 = (bf16[1024,1536]{1,0:T(8,128)(2,1)S(1)}, s32[1,768]{1,0:T(1,128)S(1)}) custom-call(s32[768]{0:T(1024)} %worker_hbm.1, s32[768]{0:T(1024)} %label_hbm.1, bf16[768,1024]{1,0:T(8,128)(2,1)} %emb_hbm.1), custom_call_target="tpu_custom_call" | custom-call | tf_op jit(solution)/shard_map/pack/pallas_call | solution.py:238
  4.5 53.4 %all_to_all.10 = bf16[128,8,1536]{2,1,0:T(8,128)(2,1)S(1)} all-to-all(bf16[128,8,1536]{2,1,0:T(8,128)(2,1)S(1)} %bitcast.7), channel_id=1, replica_groups=mesh['shard'=32,'grp'=4] {'shard','grp'}, dimensions={0} | all-to-all | bytes 6291456 | tf_op jit(solution)/shard_map/all_to_all | solution.py:229
  57.8 2.1 %score.1 = f32[128,128]{1,0:T(8,128)S(1)} custom-call(bf16[1024,1536]{1,0:T(8,128)(2,1)S(1)} %bitcast.6), custom_call_target="tpu_custom_call" | custom-call | tf_op jit(solution)/shard_map/score/pallas_call | solution.py:253
  60.0 13.0 %all_to_all.11 = f32[128,1,128]{2,1,0:T(1,128)S(1)} all-to-all(f32[128,1,128]{2,1,0:T(1,128)S(1)} %bitcast.8), channel_id=1, replica_groups=mesh['shard'=32,'grp'=4] {'shard','grp'}, dimensions={0} | all-to-all | bytes 131072 | tf_op jit(solution)/shard_map/all_to_all | solution.py:229
  73.0 0.9 %unpack.1 = f32[768]{0:T(1024)} custom-call(s32[1,768]{1,0:T(1,128)S(1)} %get-tuple-element.7.place_ref, f32[128,128]{1,0:T(8,128)S(1)} %bitcast.9), custom_call_target="tpu_custom_call" | custom-call | tf_op jit(solution)/shard_map/unpack/pallas_call | solution.py:263

commit v4 on v3

--- a/solution.py
+++ b/solution.py
@@ -62,14 +62,18 @@
     fetches = [
         pltpu.make_async_copy(worker_hbm, worker_ref, arrived.at[0]),
         pltpu.make_async_copy(label_hbm, label_ref, arrived.at[1]),
-        pltpu.make_async_copy(emb_hbm, emb, arrived.at[2]),
     ]
-    for fetch in fetches:
+    bands = [(0, 256), (256, 512)]
+    for i, (start, size) in enumerate(bands):
+        at = pl.ds(start, size)
+        fetches.append(pltpu.make_async_copy(emb_hbm.at[at], emb.at[at], arrived.at[2 + i]))
+    for fetch in fetches[:3]:
         fetch.start()
     before = one_hot(iota((BLOCK, BLOCK), 0) < iota((BLOCK, BLOCK), 1))
     ones = jnp.ones((BLOCK, 128), BF16)
     line = small(iota((BLOCK, rows), 0))
-    first_lane = iota((BLOCK, 128), 1) == 0
+    for fetch in fetches[3:]:
+        fetch.start()
     fetches[0].wait()
     fetches[1].wait()
     worker = worker_ref[...].reshape(1, rows)
@@ -95,40 +99,65 @@
     upper = (worker >= pairs).astype(jnp.int32)
     left_row = jnp.where(rank < WHOLE, -1, late_row + upper * 4)
     right_row = jnp.where(rank < WHOLE, -1, late_row + (1 - upper) * 4)
-    fetches[2].wait()
-
     def chosen(block, target):
         inside = target - block * BLOCK
         inside = jnp.where((inside >= 0) & (inside < BLOCK), inside, -1)
         return jnp.where(line == small(inside), jnp.ones((), BF16), jnp.zeros((), BF16))
 
-    def empty(spread, counts, slot):
-        return jnp.where(first_lane & (dot(one_hot(spread), counts) <= slot.astype(F32)), MARK, 0.0)
+    lane = iota((1, 128), 1)
+
+    def filled(spread, counts):
+        each = 128 // len(counts)
+        merged = counts[0]
+        for b in range(1, len(counts)):
+            merged = jnp.where(small(lane) < small(jnp.full_like(lane, b * each)), merged, counts[b])
+        return dot(one_hot(spread), merged)
+
+    def empty(block, blocks, filled, slot):
+        return jnp.where((lane == block * (128 // blocks)) & (filled <= slot.astype(F32)), MARK, 0.0)
+
+    late_blocks = range(pairs * 8 // BLOCK)
+    jobs = [(block, target, k * half, half) for block in late_blocks for k, target in enumerate((left_row, right_row))]
+    hot = [chosen(block, target) for block, target, _, _ in jobs]
+    sums = [0.0] * len(jobs)
+    for i, (start, size) in enumerate(bands):
+        fetches[2 + i].wait()
+        for n, (_, _, column, columns) in enumerate(jobs):
+            part = dot(hot[n][:, start : start + size], emb[start : start + size, column : column + columns])
+            sums[n] = part if i == 0 else sums[n] + part
 
     r, c = iota((BLOCK, 128), 0), iota((BLOCK, 128), 1)
-    for block in range(pairs * 8 // BLOCK):
-        left = dot(chosen(block, left_row), emb[:, :half])
-        right = dot(chosen(block, right_row), emb[:, half:])
+    blocks = pairs * 8 // BLOCK
+    per_block = BLOCK // 8 * SUB
+    spread = c == (r >> 2 & 1) * per_block + (r >> 3) * SUB + (r >> 1 & 1)
+    counts = [
+        [total[at + block * per_block :][:per_block] for at in (0, clusters // 2)]
+        for block in range(blocks)
+    ]
+    late_filled = filled(spread, [jnp.concatenate(x, axis=0) for x in counts])
+    late_slot = WHOLE + (r & 1)
+    for block in range(blocks):
+        left, right = sums[2 * block], sums[2 * block + 1]
         left_sum = jnp.broadcast_to(jnp.sum(left * left, axis=1, keepdims=True), (BLOCK, 128))
         right_sum = jnp.broadcast_to(jnp.sum(right * right, axis=1, keepdims=True), (BLOCK, 128))
         left_scale = lax.rsqrt(left_sum + turned(right_sum) + 1e-06)[:, :1]
         right_scale = lax.rsqrt(right_sum + turned(left_sum) + 1e-06)[:, :1]
-        per_block = BLOCK // 8 * SUB
-        counts = [total[at + block * per_block :][:per_block] for at in (0, clusters // 2)]
-        spread = c == (r >> 2 & 1) * per_block + (r >> 3) * SUB + (r >> 1 & 1)
-        mark = empty(spread, jnp.concatenate(counts, axis=0), WHOLE + (r & 1))
+        mark = empty(block, blocks, late_filled, late_slot)
         left = left * left_scale
         left = jnp.concatenate([left[:, :128] + mark, left[:, 128:]], axis=1).astype(BF16)
         right = (right * right_scale).astype(BF16)
         out_ref[pl.ds(block * BLOCK, BLOCK), width:] = merged_rows(left, right, 4)
         out_ref[pl.ds((block + pairs * 8 // BLOCK) * BLOCK, BLOCK), width:] = merged_rows(right, left, 4)
     r, c = iota((BLOCK, BLOCK // WHOLE), 0), iota((BLOCK, BLOCK // WHOLE), 1)
-    for block in range(clusters * WHOLE // BLOCK):
+    blocks = clusters * WHOLE // BLOCK
+    counts = [total[block * BLOCK // WHOLE :][: BLOCK // WHOLE] for block in range(blocks)]
+    whole_filled = filled(c == r >> 2, counts)
+    whole_slot = iota((BLOCK, 128), 0) & 3
+    for block in range(blocks):
         at = pl.ds(block * BLOCK, BLOCK)
         values = dot(chosen(block, whole_row), emb[...])
         values = values * lax.rsqrt(jnp.sum(values * values, axis=1, keepdims=True) + 1e-06)
-        counts = total[block * BLOCK // WHOLE :][: BLOCK // WHOLE]
-        mark = empty(c == r >> 2, counts, (iota((BLOCK, 128), 0) & 3))
+        mark = empty(block, blocks, whole_filled, whole_slot)
         out_ref[at, :128] = (values[:, :128] + mark).astype(BF16)
         out_ref[at, 128:width] = values[:, 128:].astype(BF16)
 
@@ -140,15 +169,28 @@
     half = width // 2
     wholes = devices * WHOLE
 
-    for at in range(0, wholes, BLOCK):
-        lower = in_ref[at : at + BLOCK, :width]
-        upper = in_ref[wholes + at : wholes + at + BLOCK, :width]
-        members[0, at : at + BLOCK, :] = merged_rows(lower, upper, 4)
-        members[1, at : at + BLOCK, :] = merged_rows(upper, lower, 4)
     swap = upper_half()
     lates = wholes // 2
     quarters = [in_ref[k * lates : (k + 1) * lates, width:] for k in range(4)]
+    r, c = iota((BLOCK, BLOCK), 0), iota((BLOCK, BLOCK), 1)
+    itself = jnp.where(r == c, -8.0, 0.0)
+    sub, lane = iota((8, 128), 0), iota((8, 128), 1)
+    source = (lane & 15) * 8 + sub
+
+    def in_order(best, start, part, owner):
+        total = jnp.zeros((8, 128), F32)
+        for v in range(part // 16):
+            these = jnp.broadcast_to(best[:, start + v * 128 : start + (v + 1) * 128], (8, 128))
+            moved = jnp.take_along_axis(these, source, axis=1)
+            total = total + jnp.where((lane >> 4) == owner * (part // 16) + v, moved, 0.0)
+        return total
+
+    blocks = count // BLOCK
+    found = []
     for lab in range(SUB):
+        for at in range(0, wholes, BLOCK):
+            halves = [in_ref[k * wholes + at : k * wholes + at + BLOCK, :width] for k in (lab, 1 - lab)]
+            members[lab, at : at + BLOCK, :] = merged_rows(*halves, 4)
         near, far = [
             merged_rows(quarters[k + 2 * lab], quarters[k + 2 - 2 * lab], 2) for k in (0, 1)
         ]
@@ -156,25 +198,11 @@
         crossed = turned(merged_rows(far, near, 4).astype(F32)).astype(BF16)
         members[lab, wholes:, :half] = merged_rows(straight, crossed, 4, swap)
         members[lab, wholes:, half:] = merged_rows(crossed, straight, 4, swap)
-
-    r, c = iota((BLOCK, BLOCK), 0), iota((BLOCK, BLOCK), 1)
-    itself = jnp.where(r == c, -8.0, 0.0)
-    sub, lane = iota((8, 128), 0), iota((8, 128), 1)
-    source = (lane & 15) * 8 + sub
-
-    def in_order(best, start, part, owner):
-        total = jnp.zeros((8, 128), F32)
-        for v in range(part // 16):
-            these = jnp.broadcast_to(best[:, start + v * 128 : start + (v + 1) * 128], (8, 128))
-            moved = jnp.take_along_axis(these, source, axis=1)
-            total = total + jnp.where((lane >> 4) == owner * (part // 16) + v, moved, 0.0)
-        return total
-
-    blocks = count // BLOCK
-    found = []
-    for lab in range(SUB):
         parts = [members[lab, pl.ds(i * BLOCK, BLOCK), :] for i in range(blocks)]
-        absent = [jnp.where(p[:, :128].astype(F32) > MARK - 0.5, -8.0, 0.0)[:, :1] for p in parts]
+        absent = [
+            jnp.min(jnp.where(p[:, :128].astype(F32) > MARK - 0.5, -8.0, 0.0), axis=1, keepdims=True)
+            for p in parts
+        ]
         absent_row = [jnp.broadcast_to(a, (BLOCK, 128)).T[:1] for a in absent]
         down, along = [[] for _ in parts], [[] for _ in parts]
         for i in range(blocks):
@@ -244,7 +272,7 @@
             pltpu.VMEM((rows,), jnp.int32),
             pltpu.VMEM((rows,), jnp.int32),
             pltpu.VMEM((rows, width), BF16),
-            pltpu.SemaphoreType.DMA((3,)),
+            pltpu.SemaphoreType.DMA((4,)),
         ],
         compiler_params=PARAMS,
         name="pack",

time: 74 us -> 73.9 us (level)
  no operation moved by 1% of the time
where the time goes in v4:
time: 73.9 us; the launch traced here: 73.7 us
  blocking collectives  66.4 us (90%)
  Pallas kernels  7.34 us (10%)
    all_to_all x2, blocking collectives, exchange(): return lax.all_to_all(array, AXES, split_axis=0, concat_axis=0, tiled=True)  66.4 us
    pallas_call x1, Pallas kernels, local(): pl.pallas_call(pack_kernel, out_shape=(shape(packed, BF16), shape((1, row...  4.34 us
    pallas_call x1, Pallas kernels, local(): pl.pallas_call(score_kernel, out_shape=shape((devices, 128), F32), in_spe...  2.14 us

profile of v4, /device:TPU:1, one launch (start us, length us, event | category | flops | bytes accessed | tf_op | source)
XLA Modules:
  0.0 73.7 jit_solution(10159187711699760194)
XLA Ops:
  0.0 4.3 %pack.1 = (bf16[1024,1536]{1,0:T(8,128)(2,1)S(1)}, s32[1,768]{1,0:T(1,128)S(1)}) custom-call(s32[768]{0:T(1024)} %worker_hbm.1, s32[768]{0:T(1024)} %label_hbm.1, bf16[768,1024]{1,0:T(8,128)(2,1)} %emb_hbm.1), custom_call_target="tpu_custom_call" | custom-call | tf_op jit(solution)/shard_map/pack/pallas_call | solution.py:266
  4.3 53.4 %all_to_all.10 = bf16[128,8,1536]{2,1,0:T(8,128)(2,1)S(1)} all-to-all(bf16[128,8,1536]{2,1,0:T(8,128)(2,1)S(1)} %bitcast.7), channel_id=1, replica_groups=mesh['shard'=32,'grp'=4] {'shard','grp'}, dimensions={0} | all-to-all | bytes 6291456 | tf_op jit(solution)/shard_map/all_to_all | solution.py:257
  57.7 2.1 %score.1 = f32[128,128]{1,0:T(8,128)S(1)} custom-call(bf16[1024,1536]{1,0:T(8,128)(2,1)S(1)} %bitcast.6), custom_call_target="tpu_custom_call" | custom-call | tf_op jit(solution)/shard_map/score/pallas_call | solution.py:281
  59.9 13.0 %all_to_all.11 = f32[128,1,128]{2,1,0:T(1,128)S(1)} all-to-all(f32[128,1,128]{2,1,0:T(1,128)S(1)} %bitcast.8), channel_id=1, replica_groups=mesh['shard'=32,'grp'=4] {'shard','grp'}, dimensions={0} | all-to-all | bytes 131072 | tf_op jit(solution)/shard_map/all_to_all | solution.py:257
  72.9 0.9 %unpack.1 = f32[768]{0:T(1024)} custom-call(s32[1,768]{1,0:T(1,128)S(1)} %get-tuple-element.7.place_ref, f32[128,128]{1,0:T(8,128)S(1)} %bitcast.9), custom_call_target="tpu_custom_call" | custom-call | tf_op jit(solution)/shard_map/unpack/pallas_call | solution.py:291

commit v5 on v4

--- a/solution.py
+++ b/solution.py
@@ -63,7 +63,7 @@
         pltpu.make_async_copy(worker_hbm, worker_ref, arrived.at[0]),
         pltpu.make_async_copy(label_hbm, label_ref, arrived.at[1]),
     ]
-    bands = [(0, 256), (256, 512)]
+    bands = [(0, 256), (256, 256), (512, 256)]
     for i, (start, size) in enumerate(bands):
         at = pl.ds(start, size)
         fetches.append(pltpu.make_async_copy(emb_hbm.at[at], emb.at[at], arrived.at[2 + i]))
@@ -243,7 +243,8 @@
     middle = rest.astype(BF16)
     low = (rest - middle.astype(F32)).astype(BF16)
     chosen = one_hot(iota((devices, rows), 0) == place >> 4)
-    values = dot(high, chosen) + dot(middle, chosen) + dot(low, chosen)
+    values = dot(jnp.concatenate([high, middle, low], axis=0), chosen)
+    values = values[:16] + values[16:32] + values[32:]
     mine = iota((16, rows), 0) == (place & 15)
     out_ref[...] = jnp.sum(jnp.where(mine, values, 0.0), axis=0)
 
@@ -272,7 +273,7 @@
             pltpu.VMEM((rows,), jnp.int32),
             pltpu.VMEM((rows,), jnp.int32),
             pltpu.VMEM((rows, width), BF16),
-            pltpu.SemaphoreType.DMA((4,)),
+            pltpu.SemaphoreType.DMA((5,)),
         ],
         compiler_params=PARAMS,
         name="pack",

time: 73.9 us -> 73.8 us (level)
  no operation moved by 1% of the time
where the time goes in v5:
time: 73.8 us; the launch traced here: 73.6 us
  blocking collectives  66.4 us (90%)
  Pallas kernels  7.26 us (10%)
    all_to_all x2, blocking collectives, exchange(): return lax.all_to_all(array, AXES, split_axis=0, concat_axis=0, tiled=True)  66.4 us
    pallas_call x1, Pallas kernels, local(): pl.pallas_call(pack_kernel, out_shape=(shape(packed, BF16), shape((1, row...  4.31 us
    pallas_call x1, Pallas kernels, local(): pl.pallas_call(score_kernel, out_shape=shape((devices, 128), F32), in_spe...  2.14 us

profile of v5, /device:TPU:1, one launch (start us, length us, event | category | flops | bytes accessed | tf_op | source)
XLA Modules:
  0.0 73.6 jit_solution(6194519380734118599)
XLA Ops:
  0.0 4.3 %pack.1 = (bf16[1024,1536]{1,0:T(8,128)(2,1)S(1)}, s32[1,768]{1,0:T(1,128)S(1)}) custom-call(s32[768]{0:T(1024)} %worker_hbm.1, s32[768]{0:T(1024)} %label_hbm.1, bf16[768,1024]{1,0:T(8,128)(2,1)} %emb_hbm.1), custom_call_target="tpu_custom_call" | custom-call | tf_op jit(solution)/shard_map/pack/pallas_call | solution.py:267
  4.3 53.4 %all_to_all.10 = bf16[128,8,1536]{2,1,0:T(8,128)(2,1)S(1)} all-to-all(bf16[128,8,1536]{2,1,0:T(8,128)(2,1)S(1)} %bitcast.7), channel_id=1, replica_groups=mesh['shard'=32,'grp'=4] {'shard','grp'}, dimensions={0} | all-to-all | bytes 6291456 | tf_op jit(solution)/shard_map/all_to_all | solution.py:258
  57.7 2.1 %score.1 = f32[128,128]{1,0:T(8,128)S(1)} custom-call(bf16[1024,1536]{1,0:T(8,128)(2,1)S(1)} %bitcast.6), custom_call_target="tpu_custom_call" | custom-call | tf_op jit(solution)/shard_map/score/pallas_call | solution.py:282
  59.8 13.0 %all_to_all.11 = f32[128,1,128]{2,1,0:T(1,128)S(1)} all-to-all(f32[128,1,128]{2,1,0:T(1,128)S(1)} %bitcast.8), channel_id=1, replica_groups=mesh['shard'=32,'grp'=4] {'shard','grp'}, dimensions={0} | all-to-all | bytes 131072 | tf_op jit(solution)/shard_map/all_to_all | solution.py:258
  72.8 0.8 %unpack.1 = f32[768]{0:T(1024)} custom-call(s32[1,768]{1,0:T(1,128)S(1)} %get-tuple-element.7.place_ref, f32[128,128]{1,0:T(8,128)S(1)} %bitcast.9), custom_call_target="tpu_custom_call" | custom-call | tf_op jit(solution)/shard_map/unpack/pallas_call | solution.py:292

commit v6 on v5

--- a/solution.py
+++ b/solution.py
@@ -205,9 +205,10 @@
         ]
         absent_row = [jnp.broadcast_to(a, (BLOCK, 128)).T[:1] for a in absent]
         down, along = [[] for _ in parts], [[] for _ in parts]
-        for i in range(blocks):
-            for j in range(i, blocks):
-                scores = dot_rows(parts[i], parts[j]) + absent[i]
+        for j in reversed(range(blocks)):
+            stacked = dot_rows(members[lab, : (j + 1) * BLOCK, :], parts[j])
+            for i in range(j + 1):
+                scores = stacked[i * BLOCK : (i + 1) * BLOCK] + absent[i]
                 if i == j:
                     down[j].append(scores + itself)
                 else:

time: 73.8 us -> 73.7 us (level)
  no operation moved by 1% of the time
where the time goes in v6:
time: 73.7 us; the launch traced here: 73.5 us
  blocking collectives  66.4 us (90%)
  Pallas kernels  7.17 us (10%)
    all_to_all x2, blocking collectives, exchange(): return lax.all_to_all(array, AXES, split_axis=0, concat_axis=0, tiled=True)  66.4 us
    pallas_call x1, Pallas kernels, local(): pl.pallas_call(pack_kernel, out_shape=(shape(packed, BF16), shape((1, row...  4.31 us
    pallas_call x1, Pallas kernels, local(): pl.pallas_call(score_kernel, out_shape=shape((devices, 128), F32), in_spe...  2.05 us

profile of v6, /device:TPU:1, one launch (start us, length us, event | category | flops | bytes accessed | tf_op | source)
XLA Modules:
  0.0 73.5 jit_solution(1717014436015935294)
XLA Ops:
  0.0 4.3 %pack.1 = (bf16[1024,1536]{1,0:T(8,128)(2,1)S(1)}, s32[1,768]{1,0:T(1,128)S(1)}) custom-call(s32[768]{0:T(1024)} %worker_hbm.1, s32[768]{0:T(1024)} %label_hbm.1, bf16[768,1024]{1,0:T(8,128)(2,1)} %emb_hbm.1), custom_call_target="tpu_custom_call" | custom-call | tf_op jit(solution)/shard_map/pack/pallas_call | solution.py:268
  4.3 53.4 %all_to_all.10 = bf16[128,8,1536]{2,1,0:T(8,128)(2,1)S(1)} all-to-all(bf16[128,8,1536]{2,1,0:T(8,128)(2,1)S(1)} %bitcast.7), channel_id=1, replica_groups=mesh['shard'=32,'grp'=4] {'shard','grp'}, dimensions={0} | all-to-all | bytes 6291456 | tf_op jit(solution)/shard_map/all_to_all | solution.py:259
  57.7 2.0 %score.1 = f32[128,128]{1,0:T(8,128)S(1)} custom-call(bf16[1024,1536]{1,0:T(8,128)(2,1)S(1)} %bitcast.6), custom_call_target="tpu_custom_call" | custom-call | tf_op jit(solution)/shard_map/score/pallas_call | solution.py:283
  59.7 13.0 %all_to_all.11 = f32[128,1,128]{2,1,0:T(1,128)S(1)} all-to-all(f32[128,1,128]{2,1,0:T(1,128)S(1)} %bitcast.8), channel_id=1, replica_groups=mesh['shard'=32,'grp'=4] {'shard','grp'}, dimensions={0} | all-to-all | bytes 131072 | tf_op jit(solution)/shard_map/all_to_all | solution.py:259
  72.7 0.8 %unpack.1 = f32[768]{0:T(1024)} custom-call(s32[1,768]{1,0:T(1,128)S(1)} %get-tuple-element.7.place_ref, f32[128,128]{1,0:T(8,128)S(1)} %bitcast.9), custom_call_target="tpu_custom_call" | custom-call | tf_op jit(solution)/shard_map/unpack/pallas_call | solution.py:293

commit v7 on v6

--- a/solution.py
+++ b/solution.py
@@ -186,7 +186,7 @@
         return total
 
     blocks = count // BLOCK
-    found = []
+    found, bests = [], []
     for lab in range(SUB):
         for at in range(0, wholes, BLOCK):
             halves = [in_ref[k * wholes + at : k * wholes + at + BLOCK, :width] for k in (lab, 1 - lab)]
@@ -222,7 +222,8 @@
                 other = functools.reduce(jnp.maximum, along[i]).T
                 best = jnp.maximum(best, jnp.max(other, axis=0, keepdims=True))
             merged.append(jnp.where(best < -2.0, -1.0, best))
-        best = jnp.concatenate(merged, axis=1)
+        bests.append(jnp.concatenate(merged, axis=1))
+    for lab, best in enumerate(bests):
         whole = in_order(best, 0, devices // 2, sub >> 2 ^ lab)
         whole = whole + pltpu.roll(whole, 4, 0)
         late = in_order(best, wholes, devices // 4, (sub >> 2) + ((sub >> 1 & 1) ^ lab) * 2)

time: 73.7 us -> 73.7 us (level)
  no operation moved by 1% of the time
where the time goes in v7:
time: 73.7 us; the launch traced here: 73.5 us
  blocking collectives  66.4 us (90%)
  Pallas kernels  7.17 us (10%)
    all_to_all x2, blocking collectives, exchange(): return lax.all_to_all(array, AXES, split_axis=0, concat_axis=0, tiled=True)  66.4 us
    pallas_call x1, Pallas kernels, local(): pl.pallas_call(pack_kernel, out_shape=(shape(packed, BF16), shape((1, row...  4.31 us
    pallas_call x1, Pallas kernels, local(): pl.pallas_call(score_kernel, out_shape=shape((devices, 128), F32), in_spe...  2.05 us

profile of v7, /device:TPU:1, one launch (start us, length us, event | category | flops | bytes accessed | tf_op | source)
XLA Modules:
  0.0 73.5 jit_solution(2065707078844159515)
XLA Ops:
  0.0 4.3 %pack.1 = (bf16[1024,1536]{1,0:T(8,128)(2,1)S(1)}, s32[1,768]{1,0:T(1,128)S(1)}) custom-call(s32[768]{0:T(1024)} %worker_hbm.1, s32[768]{0:T(1024)} %label_hbm.1, bf16[768,1024]{1,0:T(8,128)(2,1)} %emb_hbm.1), custom_call_target="tpu_custom_call" | custom-call | tf_op jit(solution)/shard_map/pack/pallas_call | solution.py:269
  4.3 53.4 %all_to_all.10 = bf16[128,8,1536]{2,1,0:T(8,128)(2,1)S(1)} all-to-all(bf16[128,8,1536]{2,1,0:T(8,128)(2,1)S(1)} %bitcast.7), channel_id=1, replica_groups=mesh['shard'=32,'grp'=4] {'shard','grp'}, dimensions={0} | all-to-all | bytes 6291456 | tf_op jit(solution)/shard_map/all_to_all | solution.py:260
  57.7 2.0 %score.1 = f32[128,128]{1,0:T(8,128)S(1)} custom-call(bf16[1024,1536]{1,0:T(8,128)(2,1)S(1)} %bitcast.6), custom_call_target="tpu_custom_call" | custom-call | tf_op jit(solution)/shard_map/score/pallas_call | solution.py:284
  59.7 13.0 %all_to_all.11 = f32[128,1,128]{2,1,0:T(1,128)S(1)} all-to-all(f32[128,1,128]{2,1,0:T(1,128)S(1)} %bitcast.8), channel_id=1, replica_groups=mesh['shard'=32,'grp'=4] {'shard','grp'}, dimensions={0} | all-to-all | bytes 131072 | tf_op jit(solution)/shard_map/all_to_all | solution.py:260
  72.7 0.8 %unpack.1 = f32[768]{0:T(1024)} custom-call(s32[1,768]{1,0:T(1,128)S(1)} %get-tuple-element.7.place_ref, f32[128,128]{1,0:T(8,128)S(1)} %bitcast.9), custom_call_target="tpu_custom_call" | custom-call | tf_op jit(solution)/shard_map/unpack/pallas_call | solution.py:294

commit v8 on v6

--- a/solution.py
+++ b/solution.py
@@ -188,9 +188,6 @@
     blocks = count // BLOCK
     found = []
     for lab in range(SUB):
-        for at in range(0, wholes, BLOCK):
-            halves = [in_ref[k * wholes + at : k * wholes + at + BLOCK, :width] for k in (lab, 1 - lab)]
-            members[lab, at : at + BLOCK, :] = merged_rows(*halves, 4)
         near, far = [
             merged_rows(quarters[k + 2 * lab], quarters[k + 2 - 2 * lab], 2) for k in (0, 1)
         ]
@@ -198,6 +195,9 @@
         crossed = turned(merged_rows(far, near, 4).astype(F32)).astype(BF16)
         members[lab, wholes:, :half] = merged_rows(straight, crossed, 4, swap)
         members[lab, wholes:, half:] = merged_rows(crossed, straight, 4, swap)
+        for at in range(0, wholes, BLOCK):
+            halves = [in_ref[k * wholes + at : k * wholes + at + BLOCK, :width] for k in (lab, 1 - lab)]
+            members[lab, at : at + BLOCK, :] = merged_rows(*halves, 4)
         parts = [members[lab, pl.ds(i * BLOCK, BLOCK), :] for i in range(blocks)]
         absent = [
             jnp.min(jnp.where(p[:, :128].astype(F32) > MARK - 0.5, -8.0, 0.0), axis=1, keepdims=True)

time: 73.7 us -> 73.7 us (level)
  no operation moved by 1% of the time
where the time goes in v8:
time: 73.7 us; the launch traced here: 73.5 us
  blocking collectives  66.4 us (90%)
  Pallas kernels  7.17 us (10%)
    all_to_all x2, blocking collectives, exchange(): return lax.all_to_all(array, AXES, split_axis=0, concat_axis=0, tiled=True)  66.4 us
    pallas_call x1, Pallas kernels, local(): pl.pallas_call(pack_kernel, out_shape=(shape(packed, BF16), shape((1, row...  4.31 us
    pallas_call x1, Pallas kernels, local(): pl.pallas_call(score_kernel, out_shape=shape((devices, 128), F32), in_spe...  2.05 us

profile of v8, /device:TPU:1, one launch (start us, length us, event | category | flops | bytes accessed | tf_op | source)
XLA Modules:
  0.0 73.5 jit_solution(16838713891816663352)
XLA Ops:
  0.0 4.3 %pack.1 = (bf16[1024,1536]{1,0:T(8,128)(2,1)S(1)}, s32[1,768]{1,0:T(1,128)S(1)}) custom-call(s32[768]{0:T(1024)} %worker_hbm.1, s32[768]{0:T(1024)} %label_hbm.1, bf16[768,1024]{1,0:T(8,128)(2,1)} %emb_hbm.1), custom_call_target="tpu_custom_call" | custom-call | tf_op jit(solution)/shard_map/pack/pallas_call | solution.py:268
  4.3 53.4 %all_to_all.10 = bf16[128,8,1536]{2,1,0:T(8,128)(2,1)S(1)} all-to-all(bf16[128,8,1536]{2,1,0:T(8,128)(2,1)S(1)} %bitcast.7), channel_id=1, replica_groups=mesh['shard'=32,'grp'=4] {'shard','grp'}, dimensions={0} | all-to-all | bytes 6291456 | tf_op jit(solution)/shard_map/all_to_all | solution.py:259
  57.7 2.0 %score.1 = f32[128,128]{1,0:T(8,128)S(1)} custom-call(bf16[1024,1536]{1,0:T(8,128)(2,1)S(1)} %bitcast.6), custom_call_target="tpu_custom_call" | custom-call | tf_op jit(solution)/shard_map/score/pallas_call | solution.py:283
  59.7 13.0 %all_to_all.11 = f32[128,1,128]{2,1,0:T(1,128)S(1)} all-to-all(f32[128,1,128]{2,1,0:T(1,128)S(1)} %bitcast.8), channel_id=1, replica_groups=mesh['shard'=32,'grp'=4] {'shard','grp'}, dimensions={0} | all-to-all | bytes 131072 | tf_op jit(solution)/shard_map/all_to_all | solution.py:259
  72.7 0.8 %unpack.1 = f32[768]{0:T(1024)} custom-call(s32[1,768]{1,0:T(1,128)S(1)} %get-tuple-element.7.place_ref, f32[128,128]{1,0:T(8,128)S(1)} %bitcast.9), custom_call_target="tpu_custom_call" | custom-call | tf_op jit(solution)/shard_map/unpack/pallas_call | solution.py:293
